TPU v7x, 256 devices: a whole 4x4x8 slice. The times are simulated.
256 devices in a mesh: band: 16 (over x_lo, z), dom: 16 (over y, x_hi, core).
Axes of the slice: x: 4 (x_hi: 2, x_lo: 2; x = x_hi * 2 + x_lo), y: 4, z: 8, core: 2. Of those that a mesh axis runs over, the one named last changes fastest.
Arguments:
- orbitals: float32 [64, 96, 32, 128], P('band', 'dom'), may hold values from -6 to 6
- potential: float32 [96, 32, 128], P('dom'), may hold values from -1.5 to 1.5
- support: int32 [16, 2, 48, 384], P('dom'), may hold values from 0 to 24575
- projectors: float32 [16, 2, 48, 8, 384], P('dom'), may hold values from -0.4375 to 0.4375
- slot_rows: int32 [16, 2, 48], P('dom'), may hold values from 0 to 47, each once within a row
- energies: float32 [16, 48, 8], replicated, may hold values from -3 to 3
- panel_orbitals: bfloat16 [512, 96, 32, 128], P('band', 'dom'), may hold values from -6 to 6
Outputs:
- filtered: float32 [64, 96, 32, 128], P('band', 'dom')
- correlation: float32 [64, 512], P('dom', 'band')
Inputs may be any that keep to these rules, and one draw needn't show every extreme that they name: `support`: cell numbers within the block; a cell may repeat. `slot_rows`: on each block, the home slots (index 0) name every atom row once, and so do the spilled slots (index 1); spilled slots of block b belong to atoms homed on block b - 1, cyclically.
All inputs are finite; a program needn't handle non-finite values.
Results may differ from a plain program's by a relative error of at most 0.0029.
Values may be sent and summed in bfloat16 or wider, within the bound.
A program may use at most 128 MiB of HBM per device.

v0:
```python
import math

import jax
import jax.numpy as jnp
from jax import lax
from jax.sharding import PartitionSpec as P

center_shift = 7.5
half_width = 6.5


def with_halo(block, sides, width):
    for axis, dim in sides:
        count = lax.axis_size(axis)
        forward = [(i, i + 1) for i in range(count - 1)]
        forward.append((count - 1, 0))
        backward = [(target, source) for source, target in forward]
        low = lax.ppermute(
            lax.slice_in_dim(block, block.shape[dim] - width, None, axis=dim), axis, forward
        )
        high = lax.ppermute(lax.slice_in_dim(block, 0, width, axis=dim), axis, backward)
        block = jnp.concatenate([low, block, high], axis=dim)
    return block


def passed_along(array, axis, by):
    peers = lax.axis_size(axis)
    return lax.ppermute(array, axis, [(i, (i + by) % peers) for i in range(peers)])


def tapered_stencil():
    unscaled = [
        2.0
        * (-1.0) ** (reach + 1)
        * math.sin(math.pi * reach / 8.0)
        / (math.pi * reach / 8.0 * reach * reach)
        for reach in range(1, 7)
    ]
    moment = sum((reach * reach * unscaled[reach - 1] for reach in range(1, 7)))
    side_terms = [neighbour_term / moment for neighbour_term in unscaled]
    return tuple([-2.0 * sum(side_terms)] + side_terms)


def kinetic(functions):
    stencil = tapered_stencil()
    plane_count = functions.shape[1]
    padded = with_halo(functions, (("dom", 1),), 6)
    summed = 3.0 * stencil[0] * functions
    for reach in range(1, 7):
        upper_part = lax.slice_in_dim(padded, 6 + reach, 6 + reach + plane_count, axis=1)
        lower_part = lax.slice_in_dim(padded, 6 - reach, 6 - reach + plane_count, axis=1)
        summed = summed + stencil[reach] * (upper_part + lower_part)
        for along in (2, 3):
            summed = summed + stencil[reach] * (
                jnp.roll(functions, reach, along) + jnp.roll(functions, -reach, along)
            )
    return -0.5 * summed


def nonlocal_term(functions, footprint, projector_values, home_rows, spilled_rows, own_energy):
    orbital_count = functions.shape[0]
    flattened = functions.reshape(orbital_count, -1)
    sampled = flattened[:, footprint]
    partials = jnp.einsum(
        "sajq,osaq->sajo", projector_values, sampled, precision=lax.Precision.HIGHEST
    )
    home_table = jnp.zeros_like(partials[0]).at[home_rows].set(partials[0])
    spill_table = jnp.zeros_like(partials[1]).at[spilled_rows].set(partials[1])
    returned = passed_along(spill_table, "dom", -1)
    scaled = own_energy[:, :, None] * (home_table + returned)
    previous = passed_along(scaled, "dom", 1)
    weights = jnp.stack([scaled[home_rows], previous[spilled_rows]], axis=0)
    placed = jnp.einsum(
        "sajq,sajo->osaq", projector_values, weights, precision=lax.Precision.HIGHEST
    )
    deposited = jnp.zeros_like(flattened).at[:, footprint].add(placed)
    return deposited.reshape(functions.shape)


def per_device(orbitals, potential, support, projectors, slot_rows, energies, panel_orbitals):
    orbital_count = orbitals.shape[0]
    cell_count = orbitals.shape[1] * orbitals.shape[2] * orbitals.shape[3]
    domains = lax.axis_size("dom")
    position = lax.axis_index("dom")
    footprint = support[0]
    projector_values = projectors[0]
    home_rows = slot_rows[0, 0]
    spilled_rows = slot_rows[0, 1]
    own_energy = lax.dynamic_index_in_dim(energies, position, 0, keepdims=False)

    def hamiltonian(functions):
        return (
            kinetic(functions)
            + potential[None] * functions
            + nonlocal_term(
                functions, footprint, projector_values, home_rows, spilled_rows, own_energy
            )
        )

    degree_one = (hamiltonian(orbitals) - center_shift * orbitals) / half_width
    filtered = 2.0 * (hamiltonian(degree_one) - center_shift * degree_one) / half_width - orbitals
    rounded = filtered.astype(jnp.bfloat16).reshape(orbital_count, cell_count)
    flat_panel = panel_orbitals.reshape(panel_orbitals.shape[0], cell_count)
    partial_gram = lax.dot_general(
        lax.all_gather(rounded, "band", axis=0, tiled=True),
        flat_panel,
        (((1,), (1,)), ((), ())),
        preferred_element_type=jnp.float32,
    )
    scale = float(domains * cell_count) ** (-0.5)
    correlation = lax.psum_scatter(partial_gram, "dom", scatter_dimension=0, tiled=True) * scale
    return (filtered, correlation)


def solution(mesh):
    return jax.shard_map(
        per_device,
        mesh=mesh,
        in_specs=(
            P("band", "dom", None, None),
            P("dom", None, None),
            P("dom", None, None, None),
            P("dom", None, None, None, None),
            P("dom", None, None),
            P(),
            P("band", "dom", None, None),
        ),
        out_specs=(P("band", "dom", None, None), P("dom", "band")),
        check_vma=False,
    )
```

profile of v0, /device:TPU:1, one launch (start us, length us, event | category | flops | bytes accessed | tf_op | source)
XLA Modules:
  0.0 988.5 jit_solution(8576114903013870010)
XLA Ops:
  7.2 4.2 collective-permute-start.1
  11.4 7.8 copy.40
  20.0 127.1 %gather_fusion = f32[36864,4]{1,0:T(8,128)} fusion(f32[4,24576]{0,1:T(8,128)} %bitcast.75, s32[36864]{0:T(1024)S(1)} %broadcast_clamp_fusion), kind=kCustom, calls=%fused_computation | custom fusion | bytes 1327104 | tf_op jit(solution)/shard_map/gather | solution.py:63
  147.0 10.6 %copy.41 = f32[2,48,384,4]{2,3,1,0:T(4,128)S(1)} copy(f32[2,48,384,4]{3,2,1,0:T(8,128)} %bitcast.77) | data formatting | bytes 1179648 | tf_op jit(solution)/shard_map/gather | solution.py:63
  161.9 4.5 collective-permute-start.2
  195.6 9.8 copy.42
  205.4 201.2 %scatter_custom_fusion.2 = f32[4,24576]{0,1:T(8,128)} fusion(s32[36864]{0:T(1024)} %copy-done.4, f32[36864,4]{1,0:T(8,128)} %copy.42, f32[]{:T(128)} %constant.14.clone.1), kind=kCustom, calls=%fused_computation.14 | custom fusion | flops 147456 | bytes 393728 | tf_op jit(solution)/shard_map/scatter-add | solution.py:76
  406.6 7.6 copy.43
  414.4 7.6 broadcast_multiply_fusion
  422.0 6.8 copy.44
  448.7 127.1 %gather_fusion.3 = f32[36864,4]{1,0:T(8,128)} fusion(f32[4,24576]{0,1:T(8,128)} %bitcast.74, s32[36864]{0:T(1024)S(1)} %copy-done.3), kind=kCustom, calls=%fused_computation.3 | custom fusion | bytes 1327104 | tf_op jit(solution)/shard_map/gather | solution.py:63
  575.7 10.5 %copy.45 = f32[2,48,384,4]{2,3,1,0:T(4,128)S(1)} copy(f32[2,48,384,4]{3,2,1,0:T(8,128)} %bitcast.76) | data formatting | bytes 1179648 | tf_op jit(solution)/shard_map/gather | solution.py:63
  586.3 2.2 fusion.18
  590.5 6.1 collective-permute-start.6
  597.3 3.2 collective-permute-start.5
  604.3 3.6 collective-permute-done.7
  610.0 9.8 copy.46
  619.8 201.2 %scatter_custom_fusion.5 = f32[4,24576]{0,1:T(8,128)} fusion(s32[36864]{0:T(1024)} %copy-done.4, f32[36864,4]{1,0:T(8,128)} %copy.46, f32[]{:T(128)} %constant.14.clone.1), kind=kCustom, calls=%fused_computation.12 | custom fusion | flops 147456 | bytes 393728 | tf_op jit(solution)/shard_map/scatter-add | solution.py:76
  821.0 7.6 copy.47
  828.6 8.3 fusion.124
  839.0 65.6 %all-gather.3.cloned.1.call-done = bf16[16,4,24576]{2,1,0:T(4,128)(2,1)} async-done(((bf16[1,4,24576]{2,1,0:T(4,128)(2,1)}), bf16[16,4,24576]{2,1,0:T(4,128)(2,1)}) %all-gather.3.cloned.1.call-update) | async-done | bytes 3145744 | tf_op jit(solution)/shard_map/all_gather | solution.py:105
  904.6 4.5 reshape.216
  909.1 3.7 fusion.4
  912.8 68.3 %all-reduce = f32[64,32]{1,0:T(8,128)S(1)} all-reduce(f32[64,32]{1,0:T(8,128)S(1)} %fusion.4), channel_id=2, replica_groups=mesh['band'=16,'dom'=16] {'dom'}, use_global_device_ids=true, to_apply=%region_6.7.clone | all-reduce | flops 2048 | bytes 16384
  (128 shorter events, 64.6 us)
Async XLA Ops:
  7.2 150.4 %copy-start = (f32[1,2,48,8,384]{4,3,2,1,0:T(8,128)S(1)}, f32[1,2,48,8,384]{4,3,2,1,0:T(8,128)}, u32[]{:S(2)}) copy-start(f32[1,2,48,8,384]{4,3,2,1,0:T(8,128)} %param.10) | copy-start | bytes 3538948
  7.2 12.0 %copy-start.10 = (s32[1,2,48,384]{3,2,1,0:T(8,128)S(1)}, s32[1,2,48,384]{3,2,1,0:T(8,128)}, u32[]{:S(2)}) copy-start(s32[1,2,48,384]{3,2,1,0:T(8,128)} %param.9) | copy-start | bytes 442372
  7.2 897.4 %all-gather.3.cloned.1.call-start = ((), (), s32[]{:S(2)}) async-start(), calls=%async_computation | async-start | bytes 3342336 | tf_op jit(solution)/shard_map/all_gather | solution.py:105
  7.2 407.0 %collective-permute-start.1 = (f32[4,6,32,128]{3,2,1,0:T(8,128)}, f32[4,6,32,128]{3,2,1,0:T(8,128)S(1)}, u32[]{:S(2)}, u32[]{:S(2)}) collective-permute-start(f32[4,6,32,128]{3,2,1,0:T(8,128)} %param.7), channel_id=1, source_target_pairs={{0,1},{1,2},{2,3},{3,4},{4,5},{5,6},{6,7},{7,8},{8,9},{9,10},{10,1... | collective-permute-start | bytes 1179656 | tf_op jit(solution)/shard_map/ppermute | solution.py:18
  11.4 402.9 %collective-permute-start = (f32[4,6,32,128]{3,2,1,0:T(8,128)}, f32[4,6,32,128]{3,2,1,0:T(8,128)S(1)}, u32[]{:S(2)}, u32[]{:S(2)}) collective-permute-start(f32[4,6,32,128]{3,2,1,0:T(8,128)} %param.7), channel_id=1, source_target_pairs={{1,0},{2,1},{3,2},{4,3},{5,4},{6,5},{7,6},{8,7},{9,8},{10,9},{11,1... | collective-permute-start | bytes 1179656 | tf_op jit(solution)/shard_map/ppermute | solution.py:21
  20.0 139.9 %copy-start.15 = (s32[1,2,48]{2,1,0:T(2,128)S(1)}, s32[1,2,48]{2,1,0:T(2,128)}, u32[]{:S(2)}) copy-start(s32[1,2,48]{2,1,0:T(2,128)} %param.11) | copy-start | bytes 1156
  147.0 19.4 %copy-start.1 = (f32[4,6,32,128]{3,2,1,0:T(8,128)S(1)}, f32[4,6,32,128]{3,2,1,0:T(8,128)}, u32[]{:S(2)}) copy-start(f32[4,6,32,128]{3,2,1,0:T(8,128)} %param.7) | copy-start | bytes 1179652
  159.9 32.1 %copy-start.11 = (s32[48]{0:T(128)}, s32[48]{0:T(128)S(1)}, u32[]{:S(2)}) copy-start(s32[48]{0:T(128)S(1)} %get-tuple-element.108) | copy-start | bytes 580
  161.9 29.7 %collective-permute-start.2 = (f32[48,8,4]{1,2,0:T(4,128)S(1)}, f32[48,8,4]{1,2,0:T(4,128)S(1)}, u32[]{:S(2)}, u32[]{:S(2)}) collective-permute-start(f32[48,8,4]{1,2,0:T(4,128)S(1)} %scatter_fusion.1), channel_id=1, source_target_pairs={{0,15},{1,0},{2,1},{3,2},{4,3},{5,4},{6,5},{7,6},{8,7},{9,8},{10,9... | collective-permute-start | bytes 18440 | tf_op jit(solution)/shard_map/ppermute | solution.py:28
  169.3 19.0 %copy-start.5 = (f32[6,32,128]{2,1,0:T(8,128)S(1)}, f32[6,32,128]{2,1,0:T(8,128)}, u32[]{:S(2)}) copy-start(f32[6,32,128]{2,1,0:T(8,128)} %param.8) | copy-start | bytes 294916
  189.6 4.6 copy-start.8
  191.7 1.9 collective-permute-start.3
  192.0 2.3 copy-start.13
  192.0 2.3 copy-start.14
  430.9 17.8 %copy-start.3 = (s32[36864]{0:T(1024)S(1)}, s32[36864]{0:T(1024)}, u32[]{:S(2)}) copy-start(s32[36864]{0:T(1024)} %copy-done.2) | copy-start | bytes 442372
  448.7 139.9 %copy-start.12 = (s32[48]{0:T(128)S(1)}, s32[48]{0:T(128)}, u32[]{:S(2)}) copy-start(s32[48]{0:T(128)} %copy-done.11) | copy-start | bytes 580
  575.7 26.8 %copy-start.9 = (f32[48,8]{1,0:T(8,128)S(1)}, f32[48,8]{1,0:T(8,128)}, u32[]{:S(2)}) copy-start(f32[48,8]{1,0:T(8,128)} %copy-done.8) | copy-start | bytes 4612
  590.5 12.0 %collective-permute-start.6 = (f32[48,8,4]{1,2,0:T(4,128)S(1)}, f32[48,8,4]{1,2,0:T(4,128)S(1)}, u32[]{:S(2)}, u32[]{:S(2)}) collective-permute-start(f32[48,8,4]{1,2,0:T(4,128)S(1)} %scatter_fusion.3), channel_id=1, source_target_pairs={{0,15},{1,0},{2,1},{3,2},{4,3},{5,4},{6,5},{7,6},{8,7},{9,8},{10,9... | collective-permute-start | bytes 18440 | tf_op jit(solution)/shard_map/ppermute | solution.py:28
  597.3 231.3 %collective-permute-start.4 = (f32[4,6,32,128]{3,2,1,0:T(8,128)S(1)}, f32[4,6,32,128]{3,2,1,0:T(8,128)}, u32[]{:S(2)}, u32[]{:S(2)}) collective-permute-start(f32[4,6,32,128]{3,2,1,0:T(8,128)S(1)} %get-tuple-element.4), channel_id=1, source_target_pairs={{1,0},{2,1},{3,2},{4,3},{5,4},{6,5},{7,6},{8,7},{9,8},{10,9},{11,1... | collective-permute-start | bytes 1179656 | tf_op jit(solution)/shard_map/ppermute | solution.py:21
  597.3 231.3 %collective-permute-start.5 = (f32[4,6,32,128]{3,2,1,0:T(8,128)S(1)}, f32[4,6,32,128]{3,2,1,0:T(8,128)}, u32[]{:S(2)}, u32[]{:S(2)}) collective-permute-start(f32[4,6,32,128]{3,2,1,0:T(8,128)S(1)} %get-tuple-element.4), channel_id=1, source_target_pairs={{0,1},{1,2},{2,3},{3,4},{4,5},{5,6},{6,7},{7,8},{8,9},{9,10},{10,1... | collective-permute-start | bytes 1179656 | tf_op jit(solution)/shard_map/ppermute | solution.py:18
  602.6 5.3 collective-permute-start.7
  619.8 208.8 %copy-start.6 = (f32[6,32,128]{2,1,0:T(8,128)S(1)}, f32[6,32,128]{2,1,0:T(8,128)}, u32[]{:S(2)}) copy-start(f32[6,32,128]{2,1,0:T(8,128)} %broadcast_multiply_fusion.1) | copy-start | bytes 294916
  619.8 208.9 %copy-start.7 = (f32[4,6,5,128]{3,2,1,0:T(8,128)S(1)}, f32[4,6,5,128]{3,2,1,0:T(8,128)}, u32[]{:S(2)}) copy-start(f32[4,6,5,128]{3,2,1,0:T(8,128)} %get-tuple-element.38) | copy-start | bytes 184324
  821.0 16.8 %copy-start.16 = (u32[256]{0:T(256)S(1)}, u32[256]{0:T(256)}, u32[]{:S(2)}) copy-start(u32[256]{0:T(256)} %constant.58) | copy-start | bytes 3076
  (2 other events, 1.3 us)
Sparse Core Ops, SparseCore 0:
  837.9 66.6 all-gather.2
where the time goes:
time: 993 us; the launch traced here: 988 us
  other arithmetic  420 us (42%)
  local copies, waits for them, and re-layouts  386 us (39%)
  waiting for transfers between devices  70.1 us (7%)
  blocking collectives  68.3 us (7%)
  starting transfers between devices  18.8 us (2%)
  between operations  15.1 us (2%)
  matrix products  10.9 us (1%)
    scatter-add x2, other arithmetic, nonlocal_term(): deposited = jnp.zeros_like(flattened).at[:, footprint].add(placed)  402 us
    gather x4, local copies, waits for them, and re-layouts, nonlocal_term(): sampled = flattened[:, footprint]  275 us
    unnamed x1, blocking collectives  68.3 us
    all_gather x1, waiting for transfers between devices, per_device(): lax.all_gather(rounded, 'band', axis=0, tiled=True)  65.6 us
    slice x48, local copies, waits for them, and re-layouts, kinetic(): jnp.roll(functions, reach, along) + jnp.roll(functions, -reach, along)  42.9 us
  transfers between devices with their start and end apart: 9, of which 3 were waited for; matrix products, arithmetic and copies ran while one was open for 63% of the time, Pallas kernels for 0%

commit v1 on v0

v1 whole, which is shorter than its diff:
```python
import functools
import math

import jax
import jax.numpy as jnp
from jax import lax
from jax.experimental import pallas as pl
from jax.experimental.pallas import tpu as pltpu
from jax.sharding import PartitionSpec as P

center_shift = 7.5
half_width = 6.5

MESH = pl.DeviceIdType.MESH
I32, F32, BF16 = jnp.int32, jnp.float32, jnp.bfloat16
HIGHEST = lax.Precision.HIGHEST

ORB = 4
ROWS = 192
HALF = 96
PEERS = 16
ATOMS = 48
SUPP = 384
PAIRS = 24
WIDE = 2 * SUPP
CHUNK = ROWS // PEERS
PANEL_DEV = 32
NT = (((1,), (1,)), ((), ()))


def tapered_stencil():
    unscaled = [
        2.0
        * (-1.0) ** (reach + 1)
        * math.sin(math.pi * reach / 8.0)
        / (math.pi * reach / 8.0 * reach * reach)
        for reach in range(1, 7)
    ]
    moment = sum((reach * reach * unscaled[reach - 1] for reach in range(1, 7)))
    side_terms = [neighbour_term / moment for neighbour_term in unscaled]
    return tuple([-2.0 * sum(side_terms)] + side_terms)


def halo_plane(halo, o, x):
    rows = pl.ds(pl.multiple_of(o * HALF, 32) + (x % 3) * 32, 32)
    return halo[rows, (x // 3) * 128 : (x // 3) * 128 + 128].astype(F32)


def local_part(source, low, high, potential, target):
    stencil = tapered_stencil()

    def one(o, carry):
        planes = [halo_plane(low, o, x) for x in range(6)]
        planes += [source[o, x] for x in range(6)]
        planes += [halo_plane(high, o, x) for x in range(6)]
        for x in range(6):
            f = planes[6 + x]
            total = (potential[x] + (-1.5 * stencil[0] - center_shift)) * f
            for k in range(1, 7):
                around = planes[6 + x + k] + planes[6 + x - k]
                around += pltpu.roll(f, k, 0) + pltpu.roll(f, 32 - k, 0)
                around += pltpu.roll(f, k, 1) + pltpu.roll(f, 128 - k, 1)
                total += (-0.5 * stencil[k]) * around
            target[o, x] = total
        return carry

    lax.fori_loop(0, ORB, one, 0)


def to_flat(source, flat):
    for o in range(ORB):
        f = source[o].reshape(ROWS, 128).astype(BF16)
        flat[o * HALF : (o + 1) * HALF, 0:128] = f[:HALF]
        flat[o * HALF : (o + 1) * HALF, 128:256] = f[HALF:]


def build_one(s, u, support, projectors, onehot, line, values):
    t = s * PAIRS + u
    c = jnp.concatenate(
        [support[0, s, pl.ds(2 * u, 1), :], support[0, s, pl.ds(2 * u + 1, 1), :]], axis=1
    )
    values[t] = jnp.concatenate([projectors[0, s, 2 * u], projectors[0, s, 2 * u + 1]], axis=1)
    row = lax.shift_right_logical(c, 7)
    upper = (row >= HALF).astype(I32)
    line[t] = row - HALF * upper
    spot = (c & 127) + 128 * upper
    hit = lax.broadcasted_iota(I32, (256, WIDE), 0) == spot
    onehot[t] = jnp.where(hit, 1.0, 0.0).astype(BF16)


def project(s, flat, onehot, line, values, table):
    lane = lax.broadcasted_iota(I32, (8, 128), 1)

    def body(u, columns):
        t = s * PAIRS + u
        g = jnp.dot(flat[...], onehot[t], preferred_element_type=F32)
        mask = lax.broadcasted_iota(I32, (HALF, WIDE), 0) == line[t]
        p = values[t]
        out = []
        for o in range(ORB):
            picked = jnp.where(mask, g[o * HALF : (o + 1) * HALF], 0.0)
            q = p * jnp.sum(picked, axis=0, keepdims=True)
            first = jnp.sum(q[:, :SUPP], axis=1, keepdims=True)
            second = jnp.sum(q[:, SUPP:], axis=1, keepdims=True)
            column = jnp.where(lane == 2 * u, first, columns[o])
            out.append(jnp.where(lane == 2 * u + 1, second, column))
        return tuple(out)

    start = tuple(jnp.zeros((8, 128), F32) for _ in range(ORB))
    columns = lax.fori_loop(0, PAIRS, body, start, unroll=8)
    return jnp.concatenate(columns, axis=0)


def place(s, weights, onehot, line, values, total):
    lane = lax.broadcasted_iota(I32, (8, 128), 1)

    def body(u, carry):
        t = s * PAIRS + u
        mask = lax.broadcasted_iota(I32, (HALF, WIDE), 0) == line[t]
        p = values[t]
        parts = []
        for o in range(ORB):
            w = weights[s, o * 8 : (o + 1) * 8, :]
            first = jnp.sum(jnp.where(lane == 2 * u, w, 0.0), axis=1, keepdims=True)
            second = jnp.sum(jnp.where(lane == 2 * u + 1, w, 0.0), axis=1, keepdims=True)
            spread = jnp.concatenate(
                [
                    jnp.sum(p[:, :SUPP] * first, axis=0, keepdims=True),
                    jnp.sum(p[:, SUPP:] * second, axis=0, keepdims=True),
                ],
                axis=1,
            )
            parts.append(jnp.where(mask, spread, 0.0).astype(BF16))
        total[...] += lax.dot_general(
            jnp.concatenate(parts, axis=0), onehot[t], NT, preferred_element_type=F32
        )
        return carry

    lax.fori_loop(0, PAIRS, body, 0, unroll=8)


def placed_planes(total, o, x):
    rows = pl.ds(o * HALF + (x % 3) * 32, 32)
    return total[rows, (x // 3) * 128 : (x // 3) * 128 + 128]


def kernel(
    orbitals, potential, support, projectors, slot_rows, energies, panel,
    filtered, correlation,
    onehot, line, values, flat, halo_low, halo_high, table, got, weights, perm, own_slots,
    energy, local, degree_one, total, result, panel_here, ship, landed, spread_rows, gram,
    gram_out, gram_in, red, red_out, red_in,
    halo_send, halo_recv, coef_send, coef_recv, panel_send, panel_recv, keep_sem,
    ship_send, ship_recv, gram_send, gram_recv, red_send, red_recv, out_sem,
):
    band = lax.axis_index("band")
    dom = lax.axis_index("dom")
    right, left = lax.rem(dom + 1, PEERS), lax.rem(dom + PEERS - 1, PEERS)
    barrier = pltpu.get_barrier_semaphore()

    def greet(i, carry):
        pl.semaphore_signal(
            barrier, inc=1, device_id=(lax.rem(band + i, PEERS), dom), device_id_type=MESH
        )
        pl.semaphore_signal(
            barrier, inc=1, device_id=(band, lax.rem(dom + i, PEERS)), device_id_type=MESH
        )
        return carry

    lax.fori_loop(1, PEERS, greet, 0)

    to_flat(orbitals, flat.at[0])

    def build(u, carry):
        build_one(0, u, support, projectors, onehot, line, values)
        build_one(1, u, support, projectors, onehot, line, values)
        return carry

    lax.fori_loop(0, PAIRS, build, 0)
    own_slots[...] = jnp.full((2, 8, 128), -1, I32)
    energy[...] = jnp.zeros((2, 8, 128), F32)
    eye = (
        lax.broadcasted_iota(I32, (8, 8), 0) == lax.broadcasted_iota(I32, (8, 8), 1)
    ).astype(F32)
    for s, block in ((0, dom), (1, left)):
        own_slots[s, 0:1, 0:ATOMS] = slot_rows[0, s : s + 1, :]
        hit = lax.broadcasted_iota(I32, (128, 128), 0) == own_slots[s, 0:1, :]
        perm[s] = jnp.where(hit, 1.0, 0.0)
        energy[s, :, 0:ATOMS] = lax.dot_general(
            eye, energies[block], NT, precision=HIGHEST, preferred_element_type=F32
        )

    pl.semaphore_wait(barrier, 2 * (PEERS - 1))

    def to_side(source, target, send, recv, side):
        return pltpu.make_async_remote_copy(
            src_ref=source, dst_ref=target, send_sem=send, recv_sem=recv,
            device_id=(band, side), device_id_type=MESH,
        )

    def halo_copies(d):
        return (
            to_side(flat.at[d], halo_low.at[d], halo_send.at[d, 0], halo_recv.at[d, 0], right),
            to_side(flat.at[d], halo_high.at[d], halo_send.at[d, 1], halo_recv.at[d, 1], left),
        )

    def coef_copy(d, s):
        return to_side(
            table.at[d, s], got.at[d, s], coef_send.at[d, s], coef_recv.at[d, s],
            left if s else right,
        )

    def panel_copy(i):
        peer = lax.rem(band + i, PEERS)
        return pltpu.make_async_remote_copy(
            src_ref=panel.at[pl.ds(peer * CHUNK, CHUNK)],
            dst_ref=panel_here.at[:, pl.ds(pl.multiple_of(band * PANEL_DEV, PANEL_DEV), PANEL_DEV), :],
            send_sem=panel_send.at[i], recv_sem=panel_recv.at[i],
            device_id=(peer, dom), device_id_type=MESH,
        )

    keep = pltpu.make_async_copy(
        panel.at[pl.ds(band * CHUNK, CHUNK)],
        panel_here.at[:, pl.ds(pl.multiple_of(band * PANEL_DEV, PANEL_DEV), PANEL_DEV), :],
        keep_sem,
    )

    def each(copy_of, action):
        def body(i, carry):
            getattr(copy_of(i), action)()
            return carry

        lax.fori_loop(1, PEERS, body, 0)

    for copy in halo_copies(0):
        copy.start()
    keep.start()
    each(panel_copy, "start")

    def apply(d, source):
        for s in (1, 0):
            columns = project(s, flat.at[d], onehot, line, values, table)
            table[d, s] = lax.dot_general(
                columns, perm[s], NT, precision=HIGHEST, preferred_element_type=F32
            )
            coef_copy(d, s).start()
        for copy in halo_copies(d):
            copy.wait_recv()
        local_part(source, halo_low.at[d], halo_high.at[d], potential, local)
        total[...] = jnp.zeros(total.shape, F32)
        for s in (0, 1):
            coef_copy(d, 1 - s).wait_recv()
            scaled = jnp.concatenate([energy[s]] * ORB, axis=0) * (table[d, s] + got[d, 1 - s])
            weights[s] = jnp.dot(scaled, perm[s], precision=HIGHEST, preferred_element_type=F32)
            place(s, weights, onehot, line, values, total)

    apply(0, orbitals)
    for o in range(ORB):
        for x in range(6):
            degree_one[o, x] = (local[o, x] + placed_planes(total, o, x)) * (1.0 / half_width)
    to_flat(degree_one, flat.at[1])
    for copy in halo_copies(1):
        copy.start()

    apply(1, degree_one)
    for o in range(ORB):
        for x in range(6):
            new = (local[o, x] + placed_planes(total, o, x)) * (2.0 / half_width) - orbitals[o, x]
            degree_one[o, x] = new
            result[o, x * 32 : (x + 1) * 32, :] = new
    write = pltpu.make_async_copy(degree_one, filtered, out_sem)
    write.start()

    for c in range(PEERS):
        for o in range(ORB):
            spread_rows[c * ORB * CHUNK + o * CHUNK : c * ORB * CHUNK + (o + 1) * CHUNK, :] = result[
                o, c * CHUNK : (c + 1) * CHUNK, :
            ]
        ship[c] = spread_rows[c * ORB * CHUNK : (c + 1) * ORB * CHUNK, :].astype(BF16)

    def ship_copy(i):
        peer = lax.rem(band + i, PEERS)
        return pltpu.make_async_remote_copy(
            src_ref=ship.at[peer], dst_ref=landed.at[band],
            send_sem=ship_send.at[i], recv_sem=ship_recv.at[i],
            device_id=(peer, dom), device_id_type=MESH,
        )

    each(ship_copy, "start")
    landed[band] = ship[band]
    keep.wait()
    each(panel_copy, "wait_recv")
    each(ship_copy, "wait_recv")

    for c in range(PEERS):
        spread_rows[c * ORB * CHUNK : (c + 1) * ORB * CHUNK, :] = landed[c].astype(F32)
    products = jnp.zeros((ORB * PEERS, PEERS * PANEL_DEV), F32)
    for k in range(0, CHUNK, 2):
        lines = [
            jnp.concatenate(
                [
                    spread_rows[pl.ds(o * CHUNK + n, PEERS, stride=ORB * CHUNK), :]
                    for o in range(ORB)
                ],
                axis=0,
            )
            for n in (k, k + 1)
        ]
        products += lax.dot_general(
            jnp.concatenate(lines, axis=1).astype(BF16),
            jnp.concatenate([panel_here[k], panel_here[k + 1]], axis=1),
            NT,
            preferred_element_type=F32,
        )
    for n in range(4):
        gram[n] = products[:, n * 128 : (n + 1) * 128]

    for d in range(PEERS):
        for n in range(4):
            gram_out[
                d, (n // 2) * ORB : (n // 2) * ORB + ORB, (n % 2) * 128 : (n % 2) * 128 + 128
            ] = gram[n, pl.ds(d, ORB, stride=PEERS), :]

    def gram_copy(i):
        peer = lax.rem(dom + i, PEERS)
        return pltpu.make_async_remote_copy(
            src_ref=gram_out.at[peer], dst_ref=gram_in.at[dom],
            send_sem=gram_send.at[i], recv_sem=gram_recv.at[i],
            device_id=(band, peer), device_id_type=MESH,
        )

    each(gram_copy, "start")
    gram_in[dom] = gram_out[dom]
    each(gram_copy, "wait_recv")
    red[...] = jnp.sum(gram_in[...], axis=0)
    red_out[...] = jnp.zeros(red_out.shape, F32)
    for b in range(PEERS):
        half, at = b // 8, (b % 8) * PANEL_DEV
        red_out[b, 0:ORB, 0:PANEL_DEV] = red[half * ORB : (half + 1) * ORB, at : at + PANEL_DEV]

    def red_copy(i):
        peer = lax.rem(band + i, PEERS)
        return pltpu.make_async_remote_copy(
            src_ref=red_out.at[peer], dst_ref=red_in.at[band],
            send_sem=red_send.at[i], recv_sem=red_recv.at[i],
            device_id=(peer, dom), device_id_type=MESH,
        )

    each(red_copy, "start")
    red_in[band] = red_out[band]
    each(red_copy, "wait_recv")
    scale = float(PEERS * ROWS * 128) ** (-0.5)
    correlation[...] = jnp.sum(red_in[...], axis=0)[0:ORB, 0:PANEL_DEV] * scale

    write.wait()
    for d in range(2):
        for copy in halo_copies(d):
            copy.wait_send()
        for s in range(2):
            coef_copy(d, s).wait_send()
    for copy_of in (panel_copy, ship_copy, gram_copy, red_copy):
        each(copy_of, "wait_send")


def per_device(orbitals, potential, support, projectors, slot_rows, energies, panel_orbitals):
    lines = panel_orbitals.reshape(PANEL_DEV, ROWS, 128).transpose(1, 0, 2)
    vmem = pl.BlockSpec(memory_space=pltpu.VMEM)
    anywhere = pl.BlockSpec(memory_space=pl.ANY)
    dma = pltpu.SemaphoreType.DMA
    return pl.pallas_call(
        kernel,
        out_shape=(
            jax.ShapeDtypeStruct((ORB, 6, 32, 128), F32),
            jax.ShapeDtypeStruct((ORB, PANEL_DEV), F32),
        ),
        in_specs=[vmem] * 6 + [anywhere],
        out_specs=(anywhere, vmem),
        scratch_shapes=[
            pltpu.VMEM((2 * PAIRS, 256, WIDE), BF16),
            pltpu.VMEM((2 * PAIRS, 1, WIDE), I32),
            pltpu.VMEM((2 * PAIRS, 8, WIDE), F32),
            pltpu.VMEM((2, ORB * HALF, 256), BF16),
            pltpu.VMEM((2, ORB * HALF, 256), BF16),
            pltpu.VMEM((2, ORB * HALF, 256), BF16),
            pltpu.VMEM((2, 2, ORB * 8, 128), F32),
            pltpu.VMEM((2, 2, ORB * 8, 128), F32),
            pltpu.VMEM((2, ORB * 8, 128), F32),
            pltpu.VMEM((2, 128, 128), F32),
            pltpu.VMEM((2, 8, 128), I32),
            pltpu.VMEM((2, 8, 128), F32),
            pltpu.VMEM((ORB, 6, 32, 128), F32),
            pltpu.VMEM((ORB, 6, 32, 128), F32),
            pltpu.VMEM((ORB * HALF, 256), F32),
            pltpu.VMEM((ORB, ROWS, 128), F32),
            pltpu.VMEM((CHUNK, PEERS * PANEL_DEV, 128), BF16),
            pltpu.VMEM((PEERS, ORB * CHUNK, 128), BF16),
            pltpu.VMEM((PEERS, ORB * CHUNK, 128), BF16),
            pltpu.VMEM((PEERS * ORB * CHUNK, 128), F32),
            pltpu.VMEM((4, ORB * PEERS, 128), F32),
            pltpu.VMEM((PEERS, 2 * ORB, 256), F32),
            pltpu.VMEM((PEERS, 2 * ORB, 256), F32),
            pltpu.VMEM((2 * ORB, 256), F32),
            pltpu.VMEM((PEERS, 8, 128), F32),
            pltpu.VMEM((PEERS, 8, 128), F32),
            dma((2, 2)), dma((2, 2)),
            dma((2, 2)), dma((2, 2)),
            dma((PEERS,)), dma((PEERS,)), dma,
            dma((PEERS,)), dma((PEERS,)),
            dma((PEERS,)), dma((PEERS,)),
            dma((PEERS,)), dma((PEERS,)),
            dma,
        ],
        compiler_params=pltpu.CompilerParams(
            collective_id=0, has_side_effects=True, vmem_limit_bytes=60 * 2**20
        ),
    )(orbitals, potential, support, projectors, slot_rows, energies, lines)


def solution(mesh):
    return jax.shard_map(
        per_device,
        mesh=mesh,
        in_specs=(
            P("band", "dom", None, None),
            P("dom", None, None),
            P("dom", None, None, None),
            P("dom", None, None, None, None),
            P("dom", None, None),
            P(),
            P("band", "dom", None, None),
        ),
        out_specs=(P("band", "dom", None, None), P("dom", "band")),
        check_vma=False,
    )
```

time: 993 us -> 94 us (0.09)
  other arithmetic: 420 us -> 0 us
  local copies, waits for them, and re-layouts: 386 us -> 8.35 us
  Pallas kernels: 0 us -> 84.7 us
  waiting for transfers between devices: 70.1 us -> 0 us
  blocking collectives: 68.3 us -> 0 us
  starting transfers between devices: 18.8 us -> 0 us
  between operations: 15.1 us -> 0.64 us
  matrix products: 10.9 us -> 0 us
    scatter-add x2 -> x0, other arithmetic: 402 us -> none  [nonlocal_term(): deposited = jnp.zeros_like(flattened).at[:, footprint].add(placed)]
    gather x8 -> x0, local copies, waits for them, and re-layouts: 278 us -> none  [the longest x4 275 us: nonlocal_term(): sampled = flattened[:, footprint]]
    pallas_call x0 -> x1, Pallas kernels: none -> 84.7 us  [per_device(): pl.pallas_call(kernel, out_shape=(jax.ShapeDtypeStruct((ORB, 6, 32, 128),...]
    unnamed x1 -> x0, blocking collectives: 68.3 us -> none
    all_gather x1 -> x0, waiting for transfers between devices: 65.6 us -> none  [per_device(): lax.all_gather(rounded, 'band', axis=0, tiled=True)]
    slice x48 -> x0, local copies, waits for them, and re-layouts: 42.9 us -> none  [kinetic(): jnp.roll(functions, reach, along) + jnp.roll(functions, -reach, along)]
    transpose x2 -> x0, local copies, waits for them, and re-layouts: 19.6 us -> none  [nonlocal_term(): jnp.einsum('sajq,sajo->osaq', projector_values, weights, precision=lax.Pr...]
    ppermute x8 -> x0, starting transfers between devices: 18.7 us -> none  [the longest x4 11.3 us: passed_along(): lax.ppermute(array, axis, [(i, (i + by) % peers) for i in range(peers)])]
  transfers between devices with their start and end apart: 9 -> 0, of which waited for: 3 -> 0; matrix products, arithmetic and copies ran while one was open for 63% -> 0% of each run, Pallas kernels for 0% -> 0%
where the time goes in v1:
time: 94 us; the launch traced here: 93.7 us
  Pallas kernels  84.7 us (90%)
  local copies, waits for them, and re-layouts  8.35 us (9%)
    pallas_call x1, Pallas kernels, per_device(): pl.pallas_call(kernel, out_shape=(jax.ShapeDtypeStruct((ORB, 6, 32, 128),...  84.7 us
    unnamed x4, local copies, waits for them, and re-layouts  8.35 us

profile of v1, /device:TPU:1, one launch (start us, length us, event | category | flops | bytes accessed | tf_op | source)
XLA Modules:
  0.0 93.7 jit_solution(2044909088061412136)
XLA Ops:
  0.6 1.8 %copy.10.energies = f32[16,48,8]{2,1,0:T(8,128)} copy(f32[16,48,8]{1,2,0:T(8,128)} %param.12) | data formatting | bytes 49152 | tf_op args[5]
  2.4 3.6 %copy.9 = bf16[32,6,32,128]{3,0,2,1:T(8,128)(2,1)} copy(bf16[32,6,32,128]{3,2,1,0:T(8,128)(2,1)} %param.13) | data formatting | bytes 3145728 | tf_op args[6]
  6.0 84.7 %shard_map.86 = (f32[4,6,32,128]{3,2,1,0:T(8,128)}, f32[4,32]{1,0:T(4,128)}) custom-call(f32[4,6,32,128]{3,2,1,0:T(8,128)} %orbitals.1, f32[6,32,128]{2,1,0:T(8,128)} %potential.1, s32[1,2,48,384]{3,2,1,0:T(8,128)} %support.1, f32[1,2,48,8,384]{4,3,2,1,0:T(8,128)} %projectors.1, s32[1,2,48]{2,1,0:T(2,128)} %slot_rows.1, f32[16,48,8]{2,1,0:T(8,128)} %copy.10.energies, ...), custom_call_target="tpu_custom_call" | custom-call | tf_op jit(solution)/shard_map/pallas_call | solution.py:370
  90.7 1.8 %copy.13 = f32[4,6,32,128]{3,2,1,0:T(8,128)} copy(f32[4,6,32,128]{3,2,1,0:T(8,128)} %get-tuple-element.4) | data formatting | bytes 786432
  92.5 1.2 %copy.14 = f32[4,32]{1,0:T(4,128)} copy(f32[4,32]{1,0:T(4,128)} %get-tuple-element.5) | data formatting | bytes 1024

commit v2 on v1

--- a/solution.py
+++ b/solution.py
@@ -1,4 +1,3 @@
-import functools
 import math
 
 import jax
@@ -12,12 +11,14 @@
 half_width = 6.5
 
 MESH = pl.DeviceIdType.MESH
-I32, F32, BF16 = jnp.int32, jnp.float32, jnp.bfloat16
+I32, F32, BF16, F8 = jnp.int32, jnp.float32, jnp.bfloat16, jnp.float8_e4m3fn
 HIGHEST = lax.Precision.HIGHEST
 
 ORB = 4
 ROWS = 192
-HALF = 96
+STRIP = 48
+TOP = 224.0
+UNROLL = 8
 PEERS = 16
 ATOMS = 48
 SUPP = 384
@@ -41,18 +42,13 @@
     return tuple([-2.0 * sum(side_terms)] + side_terms)
 
 
-def halo_plane(halo, o, x):
-    rows = pl.ds(pl.multiple_of(o * HALF, 32) + (x % 3) * 32, 32)
-    return halo[rows, (x // 3) * 128 : (x // 3) * 128 + 128].astype(F32)
-
-
 def local_part(source, low, high, potential, target):
     stencil = tapered_stencil()
 
     def one(o, carry):
-        planes = [halo_plane(low, o, x) for x in range(6)]
+        planes = [low[o, x].astype(F32) for x in range(6)]
         planes += [source[o, x] for x in range(6)]
-        planes += [halo_plane(high, o, x) for x in range(6)]
+        planes += [high[o, x].astype(F32) for x in range(6)]
         for x in range(6):
             f = planes[6 + x]
             total = (potential[x] + (-1.5 * stencil[0] - center_shift)) * f
@@ -67,11 +63,45 @@
     lax.fori_loop(0, ORB, one, 0)
 
 
-def to_flat(source, flat):
+def two_terms(x):
+    first = x.astype(F8).astype(F32)
+    return first, x - first
+
+
+def peak(x):
+    return jnp.max(jnp.max(jnp.abs(x), axis=0, keepdims=True), axis=1, keepdims=True)
+
+
+def to_flat(source, flat, sent):
+    back, terms = [], []
     for o in range(ORB):
-        f = source[o].reshape(ROWS, 128).astype(BF16)
-        flat[o * HALF : (o + 1) * HALF, 0:128] = f[:HALF]
-        flat[o * HALF : (o + 1) * HALF, 128:256] = f[HALF:]
+        f = source[o]
+        sent[o] = f.astype(BF16)
+        top = jnp.maximum(peak(f.reshape(ROWS, 128)), 1e-30)
+        back.append(top * (1.0 / TOP))
+        terms.append(two_terms(f * (TOP / top)[None]))
+    for n in range(2):
+        for q in range(4):
+            strip = [t[n][:, 8 * q : 8 * q + 8, :].reshape(STRIP, 128) for t in terms]
+            flat[n * ORB * STRIP : (n + 1) * ORB * STRIP, q * 128 : (q + 1) * 128] = (
+                jnp.concatenate(strip, axis=0).astype(F8)
+            )
+    return back
+
+
+def onehot_of(spot):
+    wide = jnp.broadcast_to(spot, (16, WIDE))
+    upper = wide >= 256
+    low = jnp.where(upper, -1.0, wide.astype(F32)).astype(BF16)
+    high = jnp.where(upper, (wide - 256).astype(F32), -1.0).astype(BF16)
+    count = lax.broadcasted_iota(I32, (16, WIDE), 0).astype(F32).astype(BF16)
+    one, zero = jnp.array(1, BF16), jnp.array(0, BF16)
+    parts = [
+        jnp.where(count + jnp.array(16.0 * k, BF16) == side, one, zero)
+        for side in (low, high)
+        for k in range(16)
+    ]
+    return jnp.concatenate(parts, axis=0).astype(F8)
 
 
 def build_one(s, u, support, projectors, onehot, line, values):
@@ -80,35 +110,44 @@
         [support[0, s, pl.ds(2 * u, 1), :], support[0, s, pl.ds(2 * u + 1, 1), :]], axis=1
     )
     values[t] = jnp.concatenate([projectors[0, s, 2 * u], projectors[0, s, 2 * u + 1]], axis=1)
-    row = lax.shift_right_logical(c, 7)
-    upper = (row >= HALF).astype(I32)
-    line[t] = row - HALF * upper
-    spot = (c & 127) + 128 * upper
-    hit = lax.broadcasted_iota(I32, (256, WIDE), 0) == spot
-    onehot[t] = jnp.where(hit, 1.0, 0.0).astype(BF16)
-
-
-def project(s, flat, onehot, line, values, table):
+    line[t] = lax.shift_right_logical(c, 12) * 8 + (lax.shift_right_logical(c, 7) & 7)
+    hot = onehot_of((c & 127) + (lax.shift_right_logical(c, 10) & 3) * 128)
+    onehot[t] = hot
+    return hot
+
+
+def project(s, flat, onehot, line, values, build, extra):
     lane = lax.broadcasted_iota(I32, (8, 128), 1)
 
-    def body(u, columns):
+    def body(u, state):
+        columns, largest = state
         t = s * PAIRS + u
-        g = jnp.dot(flat[...], onehot[t], preferred_element_type=F32)
-        mask = lax.broadcasted_iota(I32, (HALF, WIDE), 0) == line[t]
+        if build is None:
+            hot = onehot[t]
+        else:
+            hot = build(s, u)
+        extra(s, u)
+        g = jnp.dot(flat[...], hot, preferred_element_type=F32)
+        mask = lax.broadcasted_iota(I32, (STRIP, WIDE), 0) == line[t]
         p = values[t]
+        if build is not None:
+            for n in range(6):
+                largest = jnp.maximum(largest, jnp.abs(p[:, n * 128 : (n + 1) * 128]))
         out = []
         for o in range(ORB):
-            picked = jnp.where(mask, g[o * HALF : (o + 1) * HALF], 0.0)
-            q = p * jnp.sum(picked, axis=0, keepdims=True)
+            both = (
+                g[o * STRIP : (o + 1) * STRIP]
+                + g[(ORB + o) * STRIP : (ORB + o + 1) * STRIP]
+            )
+            q = p * jnp.sum(jnp.where(mask, both, 0.0), axis=0, keepdims=True)
             first = jnp.sum(q[:, :SUPP], axis=1, keepdims=True)
             second = jnp.sum(q[:, SUPP:], axis=1, keepdims=True)
             column = jnp.where(lane == 2 * u, first, columns[o])
             out.append(jnp.where(lane == 2 * u + 1, second, column))
-        return tuple(out)
-
-    start = tuple(jnp.zeros((8, 128), F32) for _ in range(ORB))
-    columns = lax.fori_loop(0, PAIRS, body, start, unroll=8)
-    return jnp.concatenate(columns, axis=0)
+        return tuple(out), largest
+
+    start = tuple(jnp.zeros((8, 128), F32) for _ in range(ORB)), jnp.zeros((8, 128), F32)
+    return lax.fori_loop(0, PAIRS, body, start, unroll=UNROLL)
 
 
 def place(s, weights, onehot, line, values, total):
@@ -116,41 +155,55 @@
 
     def body(u, carry):
         t = s * PAIRS + u
-        mask = lax.broadcasted_iota(I32, (HALF, WIDE), 0) == line[t]
+        mask = lax.broadcasted_iota(I32, (STRIP, WIDE), 0) == line[t]
         p = values[t]
-        parts = []
+        firsts, seconds = [], []
         for o in range(ORB):
             w = weights[s, o * 8 : (o + 1) * 8, :]
-            first = jnp.sum(jnp.where(lane == 2 * u, w, 0.0), axis=1, keepdims=True)
-            second = jnp.sum(jnp.where(lane == 2 * u + 1, w, 0.0), axis=1, keepdims=True)
+            left = jnp.sum(jnp.where(lane == 2 * u, w, 0.0), axis=1, keepdims=True)
+            right = jnp.sum(jnp.where(lane == 2 * u + 1, w, 0.0), axis=1, keepdims=True)
             spread = jnp.concatenate(
                 [
-                    jnp.sum(p[:, :SUPP] * first, axis=0, keepdims=True),
-                    jnp.sum(p[:, SUPP:] * second, axis=0, keepdims=True),
+                    jnp.sum(p[:, :SUPP] * left, axis=0, keepdims=True),
+                    jnp.sum(p[:, SUPP:] * right, axis=0, keepdims=True),
                 ],
                 axis=1,
             )
-            parts.append(jnp.where(mask, spread, 0.0).astype(BF16))
-        total[...] += lax.dot_general(
-            jnp.concatenate(parts, axis=0), onehot[t], NT, preferred_element_type=F32
-        )
+            first, second = two_terms(spread)
+            firsts.append(jnp.where(mask, first, 0.0))
+            seconds.append(jnp.where(mask, second, 0.0))
+        g = lax.dot_general(
+            jnp.concatenate(firsts + seconds, axis=0).astype(F8),
+            onehot[t],
+            NT,
+            preferred_element_type=F32,
+        )
+        total[s] += g[: ORB * STRIP] + g[ORB * STRIP :]
         return carry
 
-    lax.fori_loop(0, PAIRS, body, 0, unroll=8)
-
-
-def placed_planes(total, o, x):
-    rows = pl.ds(o * HALF + (x % 3) * 32, 32)
-    return total[rows, (x // 3) * 128 : (x // 3) * 128 + 128]
+    lax.fori_loop(0, PAIRS, body, 0, unroll=UNROLL)
+
+
+def placed_planes(total, back, o, x):
+    rows = slice(o * STRIP + 8 * x, o * STRIP + 8 * x + 8)
+    return jnp.concatenate(
+        [
+            total[0, rows, q * 128 : (q + 1) * 128] * back[0][o]
+            + total[1, rows, q * 128 : (q + 1) * 128] * back[1][o]
+            for q in range(4)
+        ],
+        axis=0,
+    )
 
 
 def kernel(
     orbitals, potential, support, projectors, slot_rows, energies, panel,
-    filtered, correlation,
-    onehot, line, values, flat, halo_low, halo_high, table, got, weights, perm, own_slots,
-    energy, local, degree_one, total, result, panel_here, ship, landed, spread_rows, gram,
+    filtered, sums,
+    onehot, line, values, flat, sent, halo_low, halo_high, table, got, weights, perm, own_slots,
+    energy, local, degree_one, total, result, panel_raw, panel_wide, panel_lines, panel_here,
+    ship, landed, spread_rows, gram,
     gram_out, gram_in, red, red_out, red_in,
-    halo_send, halo_recv, coef_send, coef_recv, panel_send, panel_recv, keep_sem,
+    halo_send, halo_recv, coef_send, coef_recv, panel_send, panel_recv, keep_sem, panel_sem,
     ship_send, ship_recv, gram_send, gram_recv, red_send, red_recv, out_sem,
 ):
     band = lax.axis_index("band")
@@ -169,26 +222,17 @@
 
     lax.fori_loop(1, PEERS, greet, 0)
 
-    to_flat(orbitals, flat.at[0])
-
-    def build(u, carry):
-        build_one(0, u, support, projectors, onehot, line, values)
-        build_one(1, u, support, projectors, onehot, line, values)
-        return carry
-
-    lax.fori_loop(0, PAIRS, build, 0)
+    fetch = pltpu.make_async_copy(panel, panel_raw, panel_sem)
+    fetch.start()
+    back_one = to_flat(orbitals, flat, sent.at[0])
     own_slots[...] = jnp.full((2, 8, 128), -1, I32)
     energy[...] = jnp.zeros((2, 8, 128), F32)
-    eye = (
-        lax.broadcasted_iota(I32, (8, 8), 0) == lax.broadcasted_iota(I32, (8, 8), 1)
-    ).astype(F32)
     for s, block in ((0, dom), (1, left)):
         own_slots[s, 0:1, 0:ATOMS] = slot_rows[0, s : s + 1, :]
         hit = lax.broadcasted_iota(I32, (128, 128), 0) == own_slots[s, 0:1, :]
         perm[s] = jnp.where(hit, 1.0, 0.0)
-        energy[s, :, 0:ATOMS] = lax.dot_general(
-            eye, energies[block], NT, precision=HIGHEST, preferred_element_type=F32
-        )
+        energy[s, :, 0:ATOMS] = energies[block]
+    fetch.wait()
 
     pl.semaphore_wait(barrier, 2 * (PEERS - 1))
 
@@ -200,8 +244,8 @@
 
     def halo_copies(d):
         return (
-            to_side(flat.at[d], halo_low.at[d], halo_send.at[d, 0], halo_recv.at[d, 0], right),
-            to_side(flat.at[d], halo_high.at[d], halo_send.at[d, 1], halo_recv.at[d, 1], left),
+            to_side(sent.at[d], halo_low.at[d], halo_send.at[d, 0], halo_recv.at[d, 0], right),
+            to_side(sent.at[d], halo_high.at[d], halo_send.at[d, 1], halo_recv.at[d, 1], left),
         )
 
     def coef_copy(d, s):
@@ -213,14 +257,14 @@
     def panel_copy(i):
         peer = lax.rem(band + i, PEERS)
         return pltpu.make_async_remote_copy(
-            src_ref=panel.at[pl.ds(peer * CHUNK, CHUNK)],
+            src_ref=panel_lines.at[pl.ds(peer * CHUNK, CHUNK)],
             dst_ref=panel_here.at[:, pl.ds(pl.multiple_of(band * PANEL_DEV, PANEL_DEV), PANEL_DEV), :],
             send_sem=panel_send.at[i], recv_sem=panel_recv.at[i],
             device_id=(peer, dom), device_id_type=MESH,
         )
 
     keep = pltpu.make_async_copy(
-        panel.at[pl.ds(band * CHUNK, CHUNK)],
+        panel_lines.at[pl.ds(band * CHUNK, CHUNK)],
         panel_here.at[:, pl.ds(pl.multiple_of(band * PANEL_DEV, PANEL_DEV), PANEL_DEV), :],
         keep_sem,
     )
@@ -234,38 +278,79 @@
 
     for copy in halo_copies(0):
         copy.start()
-    keep.start()
-    each(panel_copy, "start")
-
-    def apply(d, source):
+
+    def build(s, u):
+        return build_one(s, u, support, projectors, onehot, line, values)
+
+    def turn_panel(s, u):
+        if s == 1:
+            for n in range(8):
+                plane = u * 8 + n
+                panel_wide[pl.ds(pl.multiple_of(plane * 32, 32), 32), :] = panel_raw[
+                    plane // 6, plane % 6
+                ].astype(F32)
+        else:
+            for n in range(8):
+                row = u * 8 + n
+                panel_lines[row] = panel_wide[
+                    pl.ds(row, PANEL_DEV, stride=ROWS), :
+                ].astype(BF16)
+
+    def nothing(s, u):
+        pass
+
+    def apply(d, source, back, build, extra, after, largest):
+        found = []
         for s in (1, 0):
-            columns = project(s, flat.at[d], onehot, line, values, table)
+            columns, peaks = project(s, flat, onehot, line, values, build, extra)
+            found.append(peaks)
+            columns = jnp.concatenate([columns[o] * back[o] for o in range(ORB)], axis=0)
             table[d, s] = lax.dot_general(
                 columns, perm[s], NT, precision=HIGHEST, preferred_element_type=F32
             )
             coef_copy(d, s).start()
+        after()
+        if largest is None:
+            largest = jnp.max(jnp.maximum(found[0], found[1]), axis=1, keepdims=True)
         for copy in halo_copies(d):
             copy.wait_recv()
         local_part(source, halo_low.at[d], halo_high.at[d], potential, local)
         total[...] = jnp.zeros(total.shape, F32)
+        scales = []
         for s in (0, 1):
             coef_copy(d, 1 - s).wait_recv()
             scaled = jnp.concatenate([energy[s]] * ORB, axis=0) * (table[d, s] + got[d, 1 - s])
-            weights[s] = jnp.dot(scaled, perm[s], precision=HIGHEST, preferred_element_type=F32)
+            own = jnp.dot(scaled, perm[s], precision=HIGHEST, preferred_element_type=F32)
+            scales.append([])
+            for o in range(ORB):
+                w = own[o * 8 : (o + 1) * 8, :]
+                most = jnp.sum(jnp.abs(w) * largest, axis=0, keepdims=True)
+                most = jnp.maximum(jnp.max(most, axis=1, keepdims=True), 1e-30)
+                weights[s, o * 8 : (o + 1) * 8, :] = w * (TOP / most)
+                scales[s].append(most * (1.0 / TOP))
             place(s, weights, onehot, line, values, total)
-
-    apply(0, orbitals)
+        return largest, scales
+
+    def send_panel():
+        keep.start()
+        each(panel_copy, "start")
+
+    largest, scales = apply(0, orbitals, back_one, build, turn_panel, send_panel, None)
     for o in range(ORB):
         for x in range(6):
-            degree_one[o, x] = (local[o, x] + placed_planes(total, o, x)) * (1.0 / half_width)
-    to_flat(degree_one, flat.at[1])
+            degree_one[o, x] = (local[o, x] + placed_planes(total, scales, o, x)) * (
+                1.0 / half_width
+            )
+    back_two = to_flat(degree_one, flat, sent.at[1])
     for copy in halo_copies(1):
         copy.start()
 
-    apply(1, degree_one)
+    largest, scales = apply(1, degree_one, back_two, None, nothing, lambda: None, largest)
     for o in range(ORB):
         for x in range(6):
-            new = (local[o, x] + placed_planes(total, o, x)) * (2.0 / half_width) - orbitals[o, x]
+            new = (local[o, x] + placed_planes(total, scales, o, x)) * (
+                2.0 / half_width
+            ) - orbitals[o, x]
             degree_one[o, x] = new
             result[o, x * 32 : (x + 1) * 32, :] = new
     write = pltpu.make_async_copy(degree_one, filtered, out_sem)
@@ -349,8 +434,7 @@
     each(red_copy, "start")
     red_in[band] = red_out[band]
     each(red_copy, "wait_recv")
-    scale = float(PEERS * ROWS * 128) ** (-0.5)
-    correlation[...] = jnp.sum(red_in[...], axis=0)[0:ORB, 0:PANEL_DEV] * scale
+    sums[...] = jnp.sum(red_in[...], axis=0)
 
     write.wait()
     for d in range(2):
@@ -362,26 +446,31 @@
         each(copy_of, "wait_send")
 
 
+def finish(raw, sums, filtered, correlation):
+    filtered[...] = raw[...]
+    correlation[...] = sums[0:ORB, 0:PANEL_DEV] * float(PEERS * ROWS * 128) ** (-0.5)
+
+
 def per_device(orbitals, potential, support, projectors, slot_rows, energies, panel_orbitals):
-    lines = panel_orbitals.reshape(PANEL_DEV, ROWS, 128).transpose(1, 0, 2)
     vmem = pl.BlockSpec(memory_space=pltpu.VMEM)
     anywhere = pl.BlockSpec(memory_space=pl.ANY)
     dma = pltpu.SemaphoreType.DMA
-    return pl.pallas_call(
+    raw, sums = pl.pallas_call(
         kernel,
         out_shape=(
             jax.ShapeDtypeStruct((ORB, 6, 32, 128), F32),
-            jax.ShapeDtypeStruct((ORB, PANEL_DEV), F32),
+            jax.ShapeDtypeStruct((8, 128), F32),
         ),
         in_specs=[vmem] * 6 + [anywhere],
         out_specs=(anywhere, vmem),
         scratch_shapes=[
-            pltpu.VMEM((2 * PAIRS, 256, WIDE), BF16),
+            pltpu.VMEM((2 * PAIRS, 512, WIDE), F8),
             pltpu.VMEM((2 * PAIRS, 1, WIDE), I32),
             pltpu.VMEM((2 * PAIRS, 8, WIDE), F32),
-            pltpu.VMEM((2, ORB * HALF, 256), BF16),
-            pltpu.VMEM((2, ORB * HALF, 256), BF16),
-            pltpu.VMEM((2, ORB * HALF, 256), BF16),
+            pltpu.VMEM((2 * ORB * STRIP, 512), F8),
+            pltpu.VMEM((2, ORB, 6, 32, 128), BF16),
+            pltpu.VMEM((2, ORB, 6, 32, 128), BF16),
+            pltpu.VMEM((2, ORB, 6, 32, 128), BF16),
             pltpu.VMEM((2, 2, ORB * 8, 128), F32),
             pltpu.VMEM((2, 2, ORB * 8, 128), F32),
             pltpu.VMEM((2, ORB * 8, 128), F32),
@@ -390,8 +479,11 @@
             pltpu.VMEM((2, 8, 128), F32),
             pltpu.VMEM((ORB, 6, 32, 128), F32),
             pltpu.VMEM((ORB, 6, 32, 128), F32),
-            pltpu.VMEM((ORB * HALF, 256), F32),
+            pltpu.VMEM((2, ORB * STRIP, 512), F32),
             pltpu.VMEM((ORB, ROWS, 128), F32),
+            pltpu.VMEM((PANEL_DEV, 6, 32, 128), BF16),
+            pltpu.VMEM((PANEL_DEV * ROWS, 128), F32),
+            pltpu.VMEM((ROWS, PANEL_DEV, 128), BF16),
             pltpu.VMEM((CHUNK, PEERS * PANEL_DEV, 128), BF16),
             pltpu.VMEM((PEERS, ORB * CHUNK, 128), BF16),
             pltpu.VMEM((PEERS, ORB * CHUNK, 128), BF16),
@@ -404,7 +496,7 @@
             pltpu.VMEM((PEERS, 8, 128), F32),
             dma((2, 2)), dma((2, 2)),
             dma((2, 2)), dma((2, 2)),
-            dma((PEERS,)), dma((PEERS,)), dma,
+            dma((PEERS,)), dma((PEERS,)), dma, dma,
             dma((PEERS,)), dma((PEERS,)),
             dma((PEERS,)), dma((PEERS,)),
             dma((PEERS,)), dma((PEERS,)),
@@ -413,7 +505,24 @@
         compiler_params=pltpu.CompilerParams(
             collective_id=0, has_side_effects=True, vmem_limit_bytes=60 * 2**20
         ),
-    )(orbitals, potential, support, projectors, slot_rows, energies, lines)
+    )(
+        orbitals,
+        potential,
+        support,
+        projectors,
+        slot_rows,
+        energies.transpose(0, 2, 1),
+        panel_orbitals,
+    )
+    return pl.pallas_call(
+        finish,
+        out_shape=(
+            jax.ShapeDtypeStruct((ORB, 6, 32, 128), F32),
+            jax.ShapeDtypeStruct((ORB, PANEL_DEV), F32),
+        ),
+        in_specs=[vmem] * 2,
+        out_specs=(vmem, vmem),
+    )(raw, sums)
 
 
 def solution(mesh):

time: 94 us -> 87 us (0.926)
  local copies, waits for them, and re-layouts: 8.35 us -> 0 us
  Pallas kernels: 84.7 us -> 86.3 us
    unnamed x4 -> x0, local copies, waits for them, and re-layouts: 8.35 us -> none
    pallas_call x0 -> x1, Pallas kernels: none -> 1.77 us  [per_device(): pl.pallas_call(finish, out_shape=(jax.ShapeDtypeStruct((ORB, 6, 32, 128),...]
where the time goes in v2:
time: 87 us; the launch traced here: 86.9 us
  Pallas kernels  86.3 us (99%)
    pallas_call x1, Pallas kernels, per_device(): pl.pallas_call(kernel, out_shape=(jax.ShapeDtypeStruct((ORB, 6, 32, 128),...  84.5 us
    pallas_call x1, Pallas kernels, per_device(): pl.pallas_call(finish, out_shape=(jax.ShapeDtypeStruct((ORB, 6, 32, 128),...  1.77 us

profile of v2, /device:TPU:1, one launch (start us, length us, event | category | flops | bytes accessed | tf_op | source)
XLA Modules:
  0.0 86.9 jit_solution(17249280461303908864)
XLA Ops:
  0.6 84.5 %shard_map.86 = (f32[4,6,32,128]{3,2,1,0:T(8,128)}, f32[8,128]{1,0:T(8,128)}) custom-call(f32[4,6,32,128]{3,2,1,0:T(8,128)} %orbitals.1, f32[6,32,128]{2,1,0:T(8,128)} %potential.1, s32[1,2,48,384]{3,2,1,0:T(8,128)} %support.1, f32[1,2,48,8,384]{4,3,2,1,0:T(8,128)} %projectors.1, s32[1,2,48]{2,1,0:T(2,128)} %slot_rows.1, f32[16,8,48]{2,1,0:T(8,128)} %bitcast.1, ...), custom_call_target="tpu_custom_call" | custom-call | tf_op jit(solution)/shard_map/pallas_call | solution.py:458
  85.1 1.8 %shard_map.87 = (f32[4,6,32,128]{3,2,1,0:T(8,128)}, f32[4,32]{1,0:T(4,128)}) custom-call(f32[4,6,32,128]{3,2,1,0:T(8,128)} %get-tuple-element.4.raw, f32[8,128]{1,0:T(8,128)} %get-tuple-element.5.sums), custom_call_target="tpu_custom_call" | custom-call | tf_op jit(solution)/shard_map/pallas_call | solution.py:517

commit v3 on v2

--- a/solution.py
+++ b/solution.py
@@ -18,7 +18,7 @@
 ROWS = 192
 STRIP = 48
 TOP = 224.0
-UNROLL = 8
+GROUP = 12
 PEERS = 16
 ATOMS = 48
 SUPP = 384
@@ -116,7 +116,17 @@
     return hot
 
 
-def project(s, flat, onehot, line, values, build, extra):
+def grouped(body, state, tick):
+    def group(g, state):
+        tick(g)
+        for n in range(GROUP):
+            state = body(g * GROUP + n, state)
+        return state
+
+    return lax.fori_loop(0, PAIRS // GROUP, group, state)
+
+
+def project(s, flat, onehot, line, values, build, tick):
     lane = lax.broadcasted_iota(I32, (8, 128), 1)
 
     def body(u, state):
@@ -126,7 +136,6 @@
             hot = onehot[t]
         else:
             hot = build(s, u)
-        extra(s, u)
         g = jnp.dot(flat[...], hot, preferred_element_type=F32)
         mask = lax.broadcasted_iota(I32, (STRIP, WIDE), 0) == line[t]
         p = values[t]
@@ -147,10 +156,10 @@
         return tuple(out), largest
 
     start = tuple(jnp.zeros((8, 128), F32) for _ in range(ORB)), jnp.zeros((8, 128), F32)
-    return lax.fori_loop(0, PAIRS, body, start, unroll=UNROLL)
-
-
-def place(s, weights, onehot, line, values, total):
+    return grouped(body, start, tick)
+
+
+def place(s, weights, onehot, line, values, total, tick):
     lane = lax.broadcasted_iota(I32, (8, 128), 1)
 
     def body(u, carry):
@@ -181,7 +190,7 @@
         total[s] += g[: ORB * STRIP] + g[ORB * STRIP :]
         return carry
 
-    lax.fori_loop(0, PAIRS, body, 0, unroll=UNROLL)
+    grouped(body, 0, tick)
 
 
 def placed_planes(total, back, o, x):
@@ -203,7 +212,7 @@
     energy, local, degree_one, total, result, panel_raw, panel_wide, panel_lines, panel_here,
     ship, landed, spread_rows, gram,
     gram_out, gram_in, red, red_out, red_in,
-    halo_send, halo_recv, coef_send, coef_recv, panel_send, panel_recv, keep_sem, panel_sem,
+    halo_send, halo_recv, coef_send, coef_recv, panel_send, panel_recv, panel_sem,
     ship_send, ship_recv, gram_send, gram_recv, red_send, red_recv, out_sem,
 ):
     band = lax.axis_index("band")
@@ -232,8 +241,18 @@
         hit = lax.broadcasted_iota(I32, (128, 128), 0) == own_slots[s, 0:1, :]
         perm[s] = jnp.where(hit, 1.0, 0.0)
         energy[s, :, 0:ATOMS] = energies[block]
+
     fetch.wait()
 
+    def widen(u, carry):
+        for n in range(8):
+            plane = u * 8 + n
+            panel_wide[pl.ds(pl.multiple_of(plane * 32, 32), 32), :] = panel_raw[
+                plane // 6, plane % 6
+            ].astype(F32)
+        return carry
+
+    lax.fori_loop(0, PANEL_DEV * 6 // 8, widen, 0)
     pl.semaphore_wait(barrier, 2 * (PEERS - 1))
 
     def to_side(source, target, send, recv, side):
@@ -263,12 +282,6 @@
             device_id=(peer, dom), device_id_type=MESH,
         )
 
-    keep = pltpu.make_async_copy(
-        panel_lines.at[pl.ds(band * CHUNK, CHUNK)],
-        panel_here.at[:, pl.ds(pl.multiple_of(band * PANEL_DEV, PANEL_DEV), PANEL_DEV), :],
-        keep_sem,
-    )
-
     def each(copy_of, action):
         def body(i, carry):
             getattr(copy_of(i), action)()
@@ -279,37 +292,44 @@
     for copy in halo_copies(0):
         copy.start()
 
+    def send_panel(j):
+        near = (j + 1) // 2
+        i = near + (1 - j % 2) * (PEERS - 2 * near)
+        peer = lax.rem(band + i, PEERS)
+        for n in range(CHUNK):
+            row = peer * CHUNK + n
+            panel_lines[row] = panel_wide[pl.ds(row, PANEL_DEV, stride=ROWS), :].astype(BF16)
+        panel_copy(i).start()
+
+    steps = PAIRS // GROUP
+    early = PEERS - 1 - 6 * steps
+    for j in range(1, 1 + early):
+        send_panel(j)
+
+    def tick_of(stage):
+        if stage < 6:
+            return lambda g: send_panel(1 + early + stage * steps + g)
+        return lambda g: None
+
+    for n in range(CHUNK):
+        row = band * CHUNK + n
+        own = pl.ds(pl.multiple_of(band * PANEL_DEV, PANEL_DEV), PANEL_DEV)
+        panel_here[n, own, :] = panel_wide[pl.ds(row, PANEL_DEV, stride=ROWS), :].astype(BF16)
+
     def build(s, u):
         return build_one(s, u, support, projectors, onehot, line, values)
 
-    def turn_panel(s, u):
-        if s == 1:
-            for n in range(8):
-                plane = u * 8 + n
-                panel_wide[pl.ds(pl.multiple_of(plane * 32, 32), 32), :] = panel_raw[
-                    plane // 6, plane % 6
-                ].astype(F32)
-        else:
-            for n in range(8):
-                row = u * 8 + n
-                panel_lines[row] = panel_wide[
-                    pl.ds(row, PANEL_DEV, stride=ROWS), :
-                ].astype(BF16)
-
-    def nothing(s, u):
-        pass
-
-    def apply(d, source, back, build, extra, after, largest):
+    def apply(d, source, back, build, largest):
         found = []
-        for s in (1, 0):
-            columns, peaks = project(s, flat, onehot, line, values, build, extra)
+        for n, s in enumerate((1, 0)):
+            tick = tick_of(4 * d + n)
+            columns, peaks = project(s, flat, onehot, line, values, build, tick)
             found.append(peaks)
             columns = jnp.concatenate([columns[o] * back[o] for o in range(ORB)], axis=0)
             table[d, s] = lax.dot_general(
                 columns, perm[s], NT, precision=HIGHEST, preferred_element_type=F32
             )
             coef_copy(d, s).start()
-        after()
         if largest is None:
             largest = jnp.max(jnp.maximum(found[0], found[1]), axis=1, keepdims=True)
         for copy in halo_copies(d):
@@ -328,14 +348,10 @@
                 most = jnp.maximum(jnp.max(most, axis=1, keepdims=True), 1e-30)
                 weights[s, o * 8 : (o + 1) * 8, :] = w * (TOP / most)
                 scales[s].append(most * (1.0 / TOP))
-            place(s, weights, onehot, line, values, total)
+            place(s, weights, onehot, line, values, total, tick_of(4 * d + 2 + s))
         return largest, scales
 
-    def send_panel():
-        keep.start()
-        each(panel_copy, "start")
-
-    largest, scales = apply(0, orbitals, back_one, build, turn_panel, send_panel, None)
+    largest, scales = apply(0, orbitals, back_one, build, None)
     for o in range(ORB):
         for x in range(6):
             degree_one[o, x] = (local[o, x] + placed_planes(total, scales, o, x)) * (
@@ -345,7 +361,7 @@
     for copy in halo_copies(1):
         copy.start()
 
-    largest, scales = apply(1, degree_one, back_two, None, nothing, lambda: None, largest)
+    largest, scales = apply(1, degree_one, back_two, None, largest)
     for o in range(ORB):
         for x in range(6):
             new = (local[o, x] + placed_planes(total, scales, o, x)) * (
@@ -373,7 +389,6 @@
 
     each(ship_copy, "start")
     landed[band] = ship[band]
-    keep.wait()
     each(panel_copy, "wait_recv")
     each(ship_copy, "wait_recv")
 
@@ -496,7 +511,7 @@
             pltpu.VMEM((PEERS, 8, 128), F32),
             dma((2, 2)), dma((2, 2)),
             dma((2, 2)), dma((2, 2)),
-            dma((PEERS,)), dma((PEERS,)), dma, dma,
+            dma((PEERS,)), dma((PEERS,)), dma,
             dma((PEERS,)), dma((PEERS,)),
             dma((PEERS,)), dma((PEERS,)),
             dma((PEERS,)), dma((PEERS,)),

time: 87 us -> 83.7 us (0.962)
  Pallas kernels: 86.3 us -> 82.9 us
    pallas_call x1, Pallas kernels: 84.5 us -> 81.1 us  [per_device(): pl.pallas_call(kernel, out_shape=(jax.ShapeDtypeStruct((ORB, 6, 32, 128),...]
where the time goes in v3:
time: 83.7 us; the launch traced here: 83.5 us
  Pallas kernels  82.9 us (99%)
    pallas_call x1, Pallas kernels, per_device(): pl.pallas_call(kernel, out_shape=(jax.ShapeDtypeStruct((ORB, 6, 32, 128),...  81.1 us
    pallas_call x1, Pallas kernels, per_device(): pl.pallas_call(finish, out_shape=(jax.ShapeDtypeStruct((ORB, 6, 32, 128),...  1.77 us

profile of v3, /device:TPU:1, one launch (start us, length us, event | category | flops | bytes accessed | tf_op | source)
XLA Modules:
  0.0 83.5 jit_solution(8423482108611917708)
XLA Ops:
  0.6 81.1 %shard_map.86 = (f32[4,6,32,128]{3,2,1,0:T(8,128)}, f32[8,128]{1,0:T(8,128)}) custom-call(f32[4,6,32,128]{3,2,1,0:T(8,128)} %orbitals.1, f32[6,32,128]{2,1,0:T(8,128)} %potential.1, s32[1,2,48,384]{3,2,1,0:T(8,128)} %support.1, f32[1,2,48,8,384]{4,3,2,1,0:T(8,128)} %projectors.1, s32[1,2,48]{2,1,0:T(2,128)} %slot_rows.1, f32[16,8,48]{2,1,0:T(8,128)} %bitcast.1, ...), custom_call_target="tpu_custom_call" | custom-call | tf_op jit(solution)/shard_map/pallas_call | solution.py:473
  81.8 1.8 %shard_map.87 = (f32[4,6,32,128]{3,2,1,0:T(8,128)}, f32[4,32]{1,0:T(4,128)}) custom-call(f32[4,6,32,128]{3,2,1,0:T(8,128)} %get-tuple-element.4.raw, f32[8,128]{1,0:T(8,128)} %get-tuple-element.5.sums), custom_call_target="tpu_custom_call" | custom-call | tf_op jit(solution)/shard_map/pallas_call | solution.py:532

commit v4 on v3

--- a/solution.py
+++ b/solution.py
@@ -12,7 +12,6 @@
 
 MESH = pl.DeviceIdType.MESH
 I32, F32, BF16, F8 = jnp.int32, jnp.float32, jnp.bfloat16, jnp.float8_e4m3fn
-HIGHEST = lax.Precision.HIGHEST
 
 ORB = 4
 ROWS = 192
@@ -27,6 +26,7 @@
 CHUNK = ROWS // PEERS
 PANEL_DEV = 32
 NT = (((1,), (1,)), ((), ()))
+NN = (((1,), (0,)), ((), ()))
 
 
 def tapered_stencil():
@@ -159,6 +159,16 @@
     return grouped(body, start, tick)
 
 
+def permuted(x, perm, dims):
+    parts = []
+    for n in range(3):
+        parts.append(x.astype(BF16))
+        x = x - parts[n].astype(F32)
+    y = lax.dot_general(jnp.concatenate(parts, axis=0), perm, dims, preferred_element_type=F32)
+    rows = x.shape[0]
+    return y[:rows] + y[rows : 2 * rows] + y[2 * rows :]
+
+
 def place(s, weights, onehot, line, values, total, tick):
     lane = lax.broadcasted_iota(I32, (8, 128), 1)
 
@@ -209,7 +219,7 @@
     orbitals, potential, support, projectors, slot_rows, energies, panel,
     filtered, sums,
     onehot, line, values, flat, sent, halo_low, halo_high, table, got, weights, perm, own_slots,
-    energy, local, degree_one, total, result, panel_raw, panel_wide, panel_lines, panel_here,
+    energy, local, degree_one, total, result, panel_raw, panel_lines, panel_here,
     ship, landed, spread_rows, gram,
     gram_out, gram_in, red, red_out, red_in,
     halo_send, halo_recv, coef_send, coef_recv, panel_send, panel_recv, panel_sem,
@@ -239,20 +249,18 @@
     for s, block in ((0, dom), (1, left)):
         own_slots[s, 0:1, 0:ATOMS] = slot_rows[0, s : s + 1, :]
         hit = lax.broadcasted_iota(I32, (128, 128), 0) == own_slots[s, 0:1, :]
-        perm[s] = jnp.where(hit, 1.0, 0.0)
+        perm[s] = jnp.where(hit, 1.0, 0.0).astype(BF16)
         energy[s, :, 0:ATOMS] = energies[block]
 
     fetch.wait()
 
-    def widen(u, carry):
-        for n in range(8):
-            plane = u * 8 + n
-            panel_wide[pl.ds(pl.multiple_of(plane * 32, 32), 32), :] = panel_raw[
-                plane // 6, plane % 6
-            ].astype(F32)
+    def turn(x, carry):
+        for y in (0, 16):
+            lines = jnp.swapaxes(panel_raw[:, x, y : y + 16, :], 0, 1)
+            panel_lines[pl.ds(pl.multiple_of(x * 32 + y, 16), 16)] = lines
         return carry
 
-    lax.fori_loop(0, PANEL_DEV * 6 // 8, widen, 0)
+    lax.fori_loop(0, 6, turn, 0)
     pl.semaphore_wait(barrier, 2 * (PEERS - 1))
 
     def to_side(source, target, send, recv, side):
@@ -295,10 +303,6 @@
     def send_panel(j):
         near = (j + 1) // 2
         i = near + (1 - j % 2) * (PEERS - 2 * near)
-        peer = lax.rem(band + i, PEERS)
-        for n in range(CHUNK):
-            row = peer * CHUNK + n
-            panel_lines[row] = panel_wide[pl.ds(row, PANEL_DEV, stride=ROWS), :].astype(BF16)
         panel_copy(i).start()
 
     steps = PAIRS // GROUP
@@ -312,9 +316,8 @@
         return lambda g: None
 
     for n in range(CHUNK):
-        row = band * CHUNK + n
         own = pl.ds(pl.multiple_of(band * PANEL_DEV, PANEL_DEV), PANEL_DEV)
-        panel_here[n, own, :] = panel_wide[pl.ds(row, PANEL_DEV, stride=ROWS), :].astype(BF16)
+        panel_here[n, own, :] = panel_lines[band * CHUNK + n]
 
     def build(s, u):
         return build_one(s, u, support, projectors, onehot, line, values)
@@ -326,9 +329,7 @@
             columns, peaks = project(s, flat, onehot, line, values, build, tick)
             found.append(peaks)
             columns = jnp.concatenate([columns[o] * back[o] for o in range(ORB)], axis=0)
-            table[d, s] = lax.dot_general(
-                columns, perm[s], NT, precision=HIGHEST, preferred_element_type=F32
-            )
+            table[d, s] = permuted(columns, perm[s], NT)
             coef_copy(d, s).start()
         if largest is None:
             largest = jnp.max(jnp.maximum(found[0], found[1]), axis=1, keepdims=True)
@@ -340,7 +341,7 @@
         for s in (0, 1):
             coef_copy(d, 1 - s).wait_recv()
             scaled = jnp.concatenate([energy[s]] * ORB, axis=0) * (table[d, s] + got[d, 1 - s])
-            own = jnp.dot(scaled, perm[s], precision=HIGHEST, preferred_element_type=F32)
+            own = permuted(scaled, perm[s], NN)
             scales.append([])
             for o in range(ORB):
                 w = own[o * 8 : (o + 1) * 8, :]
@@ -489,7 +490,7 @@
             pltpu.VMEM((2, 2, ORB * 8, 128), F32),
             pltpu.VMEM((2, 2, ORB * 8, 128), F32),
             pltpu.VMEM((2, ORB * 8, 128), F32),
-            pltpu.VMEM((2, 128, 128), F32),
+            pltpu.VMEM((2, 128, 128), BF16),
             pltpu.VMEM((2, 8, 128), I32),
             pltpu.VMEM((2, 8, 128), F32),
             pltpu.VMEM((ORB, 6, 32, 128), F32),
@@ -497,7 +498,6 @@
             pltpu.VMEM((2, ORB * STRIP, 512), F32),
             pltpu.VMEM((ORB, ROWS, 128), F32),
             pltpu.VMEM((PANEL_DEV, 6, 32, 128), BF16),
-            pltpu.VMEM((PANEL_DEV * ROWS, 128), F32),
             pltpu.VMEM((ROWS, PANEL_DEV, 128), BF16),
             pltpu.VMEM((CHUNK, PEERS * PANEL_DEV, 128), BF16),
             pltpu.VMEM((PEERS, ORB * CHUNK, 128), BF16),

time: 83.7 us -> 80.7 us (0.964)
  Pallas kernels: 82.9 us -> 79.8 us
    pallas_call x1, Pallas kernels: 81.1 us -> 78.1 us  [per_device(): pl.pallas_call(kernel, out_shape=(jax.ShapeDtypeStruct((ORB, 6, 32, 128),...]
where the time goes in v4:
time: 80.7 us; the launch traced here: 80.5 us
  Pallas kernels  79.8 us (99%)
    pallas_call x1, Pallas kernels, per_device(): pl.pallas_call(kernel, out_shape=(jax.ShapeDtypeStruct((ORB, 6, 32, 128),...  78.1 us
    pallas_call x1, Pallas kernels, per_device(): pl.pallas_call(finish, out_shape=(jax.ShapeDtypeStruct((ORB, 6, 32, 128),...  1.77 us

profile of v4, /device:TPU:1, one launch (start us, length us, event | category | flops | bytes accessed | tf_op | source)
XLA Modules:
  0.0 80.5 jit_solution(6448483203227609943)
XLA Ops:
  0.6 78.1 %shard_map.86 = (f32[4,6,32,128]{3,2,1,0:T(8,128)}, f32[8,128]{1,0:T(8,128)}) custom-call(f32[4,6,32,128]{3,2,1,0:T(8,128)} %orbitals.1, f32[6,32,128]{2,1,0:T(8,128)} %potential.1, s32[1,2,48,384]{3,2,1,0:T(8,128)} %support.1, f32[1,2,48,8,384]{4,3,2,1,0:T(8,128)} %projectors.1, s32[1,2,48]{2,1,0:T(2,128)} %slot_rows.1, f32[16,8,48]{2,1,0:T(8,128)} %bitcast.1, ...), custom_call_target="tpu_custom_call" | custom-call | tf_op jit(solution)/shard_map/pallas_call | solution.py:474
  78.7 1.8 %shard_map.87 = (f32[4,6,32,128]{3,2,1,0:T(8,128)}, f32[4,32]{1,0:T(4,128)}) custom-call(f32[4,6,32,128]{3,2,1,0:T(8,128)} %get-tuple-element.4.raw, f32[8,128]{1,0:T(8,128)} %get-tuple-element.5.sums), custom_call_target="tpu_custom_call" | custom-call | tf_op jit(solution)/shard_map/pallas_call | solution.py:532

commit v5 on v4

--- a/solution.py
+++ b/solution.py
@@ -42,25 +42,20 @@
     return tuple([-2.0 * sum(side_terms)] + side_terms)
 
 
-def local_part(source, low, high, potential, target):
+def local_part(o, source, low, high, potential, target):
     stencil = tapered_stencil()
-
-    def one(o, carry):
-        planes = [low[o, x].astype(F32) for x in range(6)]
-        planes += [source[o, x] for x in range(6)]
-        planes += [high[o, x].astype(F32) for x in range(6)]
-        for x in range(6):
-            f = planes[6 + x]
-            total = (potential[x] + (-1.5 * stencil[0] - center_shift)) * f
-            for k in range(1, 7):
-                around = planes[6 + x + k] + planes[6 + x - k]
-                around += pltpu.roll(f, k, 0) + pltpu.roll(f, 32 - k, 0)
-                around += pltpu.roll(f, k, 1) + pltpu.roll(f, 128 - k, 1)
-                total += (-0.5 * stencil[k]) * around
-            target[o, x] = total
-        return carry
-
-    lax.fori_loop(0, ORB, one, 0)
+    planes = [low[o, x].astype(F32) for x in range(6)]
+    planes += [source[o, x] for x in range(6)]
+    planes += [high[o, x].astype(F32) for x in range(6)]
+    for x in range(6):
+        f = planes[6 + x]
+        total = (potential[x] + (-1.5 * stencil[0] - center_shift)) * f
+        for k in range(1, 7):
+            around = planes[6 + x + k] + planes[6 + x - k]
+            around += pltpu.roll(f, k, 0) + pltpu.roll(f, 32 - k, 0)
+            around += pltpu.roll(f, k, 1) + pltpu.roll(f, 128 - k, 1)
+            total += (-0.5 * stencil[k]) * around
+        target[o, x] = total
 
 
 def two_terms(x):
@@ -297,6 +292,12 @@
 
         lax.fori_loop(1, PEERS, body, 0)
 
+    def far_first(copy_of, order):
+        for i in order:
+            copy_of(i).start()
+
+    along_band = (4, 12, 3, 5, 11, 13, 2, 6, 10, 14, 1, 7, 9, 15, 8)
+    along_dom = (8, 7, 9, 6, 10, 5, 11, 4, 12, 3, 13, 2, 14, 1, 15)
     for copy in halo_copies(0):
         copy.start()
 
@@ -335,9 +336,20 @@
             largest = jnp.max(jnp.maximum(found[0], found[1]), axis=1, keepdims=True)
         for copy in halo_copies(d):
             copy.wait_recv()
-        local_part(source, halo_low.at[d], halo_high.at[d], potential, local)
         total[...] = jnp.zeros(total.shape, F32)
         scales = []
+
+        def beside(s):
+            send = tick_of(4 * d + 2 + s)
+
+            def tick(g):
+                send(g)
+                for n in range(ORB // 2 // steps):
+                    o = s * (ORB // 2) + g * (ORB // 2 // steps) + n
+                    local_part(o, source, halo_low.at[d], halo_high.at[d], potential, local)
+
+            return tick
+
         for s in (0, 1):
             coef_copy(d, 1 - s).wait_recv()
             scaled = jnp.concatenate([energy[s]] * ORB, axis=0) * (table[d, s] + got[d, 1 - s])
@@ -349,7 +361,7 @@
                 most = jnp.maximum(jnp.max(most, axis=1, keepdims=True), 1e-30)
                 weights[s, o * 8 : (o + 1) * 8, :] = w * (TOP / most)
                 scales[s].append(most * (1.0 / TOP))
-            place(s, weights, onehot, line, values, total, tick_of(4 * d + 2 + s))
+            place(s, weights, onehot, line, values, total, beside(s))
         return largest, scales
 
     largest, scales = apply(0, orbitals, back_one, build, None)
@@ -388,7 +400,7 @@
             device_id=(peer, dom), device_id_type=MESH,
         )
 
-    each(ship_copy, "start")
+    far_first(ship_copy, along_band)
     landed[band] = ship[band]
     each(panel_copy, "wait_recv")
     each(ship_copy, "wait_recv")
@@ -430,7 +442,7 @@
             device_id=(band, peer), device_id_type=MESH,
         )
 
-    each(gram_copy, "start")
+    far_first(gram_copy, along_dom)
     gram_in[dom] = gram_out[dom]
     each(gram_copy, "wait_recv")
     red[...] = jnp.sum(gram_in[...], axis=0)
@@ -447,19 +459,19 @@
             device_id=(peer, dom), device_id_type=MESH,
         )
 
-    each(red_copy, "start")
+    far_first(red_copy, along_band)
     red_in[band] = red_out[band]
-    each(red_copy, "wait_recv")
-    sums[...] = jnp.sum(red_in[...], axis=0)
-
     write.wait()
     for d in range(2):
         for copy in halo_copies(d):
             copy.wait_send()
         for s in range(2):
             coef_copy(d, s).wait_send()
-    for copy_of in (panel_copy, ship_copy, gram_copy, red_copy):
+    for copy_of in (panel_copy, ship_copy, gram_copy):
         each(copy_of, "wait_send")
+    each(red_copy, "wait_recv")
+    sums[...] = jnp.sum(red_in[...], axis=0)
+    each(red_copy, "wait_send")
 
 
 def finish(raw, sums, filtered, correlation):

time: 80.7 us -> 77.2 us (0.957)
  Pallas kernels: 79.8 us -> 76.4 us
    pallas_call x1, Pallas kernels: 78.1 us -> 74.6 us  [per_device(): pl.pallas_call(kernel, out_shape=(jax.ShapeDtypeStruct((ORB, 6, 32, 128),...]
where the time goes in v5:
time: 77.2 us; the launch traced here: 77 us
  Pallas kernels  76.4 us (99%)
    pallas_call x1, Pallas kernels, per_device(): pl.pallas_call(kernel, out_shape=(jax.ShapeDtypeStruct((ORB, 6, 32, 128),...  74.6 us
    pallas_call x1, Pallas kernels, per_device(): pl.pallas_call(finish, out_shape=(jax.ShapeDtypeStruct((ORB, 6, 32, 128),...  1.77 us

profile of v5, /device:TPU:1, one launch (start us, length us, event | category | flops | bytes accessed | tf_op | source)
XLA Modules:
  0.0 77.0 jit_solution(7570292744229431796)
XLA Ops:
  0.6 74.6 %shard_map.86 = (f32[4,6,32,128]{3,2,1,0:T(8,128)}, f32[8,128]{1,0:T(8,128)}) custom-call(f32[4,6,32,128]{3,2,1,0:T(8,128)} %orbitals.1, f32[6,32,128]{2,1,0:T(8,128)} %potential.1, s32[1,2,48,384]{3,2,1,0:T(8,128)} %support.1, f32[1,2,48,8,384]{4,3,2,1,0:T(8,128)} %projectors.1, s32[1,2,48]{2,1,0:T(2,128)} %slot_rows.1, f32[16,8,48]{2,1,0:T(8,128)} %bitcast.1, ...), custom_call_target="tpu_custom_call" | custom-call | tf_op jit(solution)/shard_map/pallas_call | solution.py:486
  75.3 1.8 %shard_map.87 = (f32[4,6,32,128]{3,2,1,0:T(8,128)}, f32[4,32]{1,0:T(4,128)}) custom-call(f32[4,6,32,128]{3,2,1,0:T(8,128)} %get-tuple-element.4.raw, f32[8,128]{1,0:T(8,128)} %get-tuple-element.5.sums), custom_call_target="tpu_custom_call" | custom-call | tf_op jit(solution)/shard_map/pallas_call | solution.py:544
